TPU v7x, 32 devices: a whole 2x2x4 slice. The times are simulated.
32 devices in a mesh: cat: 16 (over z, y, core), tp: 2 (over x).
Axes of the slice: x: 2, y: 2, z: 4, core: 2. Of those that a mesh axis runs over, the one named last changes fastest.
Arguments:
- query_emb: bfloat16 [16384, 512], P('cat', 'tp'), may hold values from -100 to 100
- positive_emb: bfloat16 [16384, 512], P('cat', 'tp'), may hold values from -6 to 6
- item_hidden: bfloat16 [32768, 1024], P('cat', 'tp'), may hold values from -6 to 6
- item_weight: bfloat16 [1024, 512], P('tp'), may hold values from -0.1875 to 0.1875
- neg_blocks: int32 [64, 64], P('cat'), may hold values from 0 to 127, all different within a row
- block_home: int32 [128], replicated, may hold values from 0 to 127, each once
- sample_counts: int32 [32768], replicated, may hold values from 1 to 4096
Outputs:
- query_loss: float32 [16384], P('cat')
- query_grad: bfloat16 [16384, 512], P('cat', 'tp')
Inputs may be any that keep to these rules, and one draw needn't show every extreme that they name: `neg_blocks`: each row names 64 different catalog blocks. `block_home`: each storage position once.
All inputs are finite; a program needn't handle non-finite values.
Results may differ from a plain program's by a relative error of at most 0.012.
Values may be sent and summed in bfloat16 or wider, within the bound.
A program may use at most 192 MiB of HBM per device.

v0:
```python
import math

import jax
import jax.numpy as jnp
from jax import lax
from jax.sharding import PartitionSpec as P

BLK = 256


def merged(value, axis, join):
    pieces = jax.tree.map(lambda part: lax.all_gather(part, axis), value)
    head = jax.tree.map(lambda part: part[0], pieces)
    tail = jax.tree.map(lambda part: part[1:], pieces)
    subtotal, _ = lax.scan(lambda subtotal, piece: (join(subtotal, piece), None), head, tail)
    return subtotal


def combine_pairs(first_pair, second_pair):
    max_first, sum_first = first_pair
    max_second, sum_second = second_pair
    new_max = jnp.maximum(max_first, max_second)
    new_sum = sum_first * jnp.exp(max_first - new_max) + sum_second * jnp.exp(max_second - new_max)
    return (new_max, new_sum)


def local(query_emb, positive_emb, item_hidden, item_weight, neg_blocks, block_home, sample_counts):
    tp_count = lax.axis_size("tp")
    tp_rank = lax.axis_index("tp")
    feat_width = item_weight.shape[1]
    hid_shard = item_hidden.shape[1]
    sub_rows = BLK // tp_count
    own_rows = item_hidden.shape[0]
    own_blocks = own_rows // BLK
    reordered = (
        item_hidden.reshape(own_blocks, tp_count, sub_rows, hid_shard)
        .transpose(1, 0, 2, 3)
        .reshape(own_rows, hid_shard)
    )
    item_vec = lax.psum_scatter(
        jnp.dot(reordered, item_weight, preferred_element_type=jnp.float32),
        "tp",
        scatter_dimension=0,
        tiled=True,
    ).astype(jnp.bfloat16)
    total_blocks = block_home.shape[0]
    log_table = jnp.log(sample_counts.astype(jnp.float32)).reshape(total_blocks, tp_count, sub_rows)
    my_logq = lax.dynamic_index_in_dim(log_table, tp_rank, 1, keepdims=False)
    query_full, positive_full = (
        lax.all_gather(query_emb, "tp", axis=1, tiled=True),
        lax.all_gather(positive_emb, "tp", axis=1, tiled=True),
    )
    qblock_count = neg_blocks.shape[0]
    query_rows = query_full.reshape(qblock_count, BLK, feat_width)
    score_scale = 2.0 / math.sqrt(feat_width)
    pos_score = score_scale * jnp.sum(
        query_full.astype(jnp.float32) * positive_full.astype(jnp.float32), axis=1
    ).reshape(qblock_count, BLK)
    matches = neg_blocks[:, :, None] == jnp.arange(total_blocks, dtype=jnp.int32)[None, None, :]
    home_ids = jnp.sum(jnp.where(matches, block_home[None, None, :], 0), axis=2)
    item_table = lax.all_gather(item_vec, "cat", axis=0, tiled=True).reshape(
        total_blocks, sub_rows, feat_width
    )
    picked = item_table[home_ids].reshape(qblock_count, -1, feat_width)
    picked_q = my_logq[home_ids].reshape(qblock_count, -1)
    scores = (
        score_scale
        * jnp.einsum("gqe,gke->gqk", query_rows, picked, preferred_element_type=jnp.float32)
        - picked_q[:, None, :]
    )
    run_max = jnp.max(scores, axis=2)
    run_sum = jnp.sum(jnp.exp(scores - run_max[..., None]), axis=2)
    run_max, run_sum = merged((run_max, run_sum), "tp", combine_pairs)
    joint_max = jnp.maximum(run_max, pos_score)
    log_total = joint_max + jnp.log(
        run_sum * jnp.exp(run_max - joint_max) + jnp.exp(pos_score - joint_max)
    )
    weights = jnp.exp(scores - log_total[..., None]).astype(jnp.bfloat16)
    weighted = jnp.einsum("gqk,gke->gqe", weights, picked, preferred_element_type=jnp.float32)
    flat_sum = weighted.reshape(qblock_count * BLK, feat_width)
    grad_share = lax.psum_scatter(
        flat_sum.astype(jnp.bfloat16), "tp", scatter_dimension=1, tiled=True
    ).astype(jnp.float32)
    pos_weight = jnp.exp(pos_score - log_total).reshape(-1)
    query_grad = score_scale * (
        grad_share + (pos_weight - 1.0)[:, None] * positive_emb.astype(jnp.float32)
    )
    query_loss = (log_total - pos_score).reshape(-1)
    return (query_loss, query_grad.astype(jnp.bfloat16))


def solution(mesh):
    placed = (
        P("cat", "tp"),
        P("cat", "tp"),
        P("cat", "tp"),
        P("tp", None),
        P("cat", None),
        P(),
        P(),
    )
    return jax.shard_map(
        local, mesh=mesh, in_specs=placed, out_specs=(P("cat"), P("cat", "tp")), check_vma=False
    )
```

profile of v0, /device:TPU:0, one launch (start us, length us, event | category | flops | bytes accessed | tf_op | source)
XLA Modules:
  0.0 367.4 jit_solution(10484836771085654601)
XLA Ops:
  7.2 0.0 copy-start
  7.2 0.0 reduce-scatter.3.cloned.1.call-start
  7.2 1.8 copy.15
  9.1 0.0 copy-done
  9.1 3.2 fusion.24
  12.3 0.0 reduce-scatter.3.cloned.1.call-update
  12.3 0.0 all-gather.10.cloned.1.call-start
  12.3 0.7 all-gather.10.cloned.1.call-update
  13.0 0.0 all-gather.12.cloned.1.call-start
  13.1 0.7 all-gather.12.cloned.1.call-update
  13.8 0.0 all-gather.8.cloned.1.call-start
  13.8 55.6 %reduce-scatter.3.cloned.1.call-done = f32[1024,512]{1,0:T(8,128)} async-done(((f32[2048,512]{1,0:T(8,128)}), f32[1024,512]{1,0:T(8,128)}) %reduce-scatter.3.cloned.1.call-update) | async-done | bytes 2097168 | tf_op jit(solution)/shard_map/reduce_scatter | solution.py:40
  69.4 2.7 convert_element_type.30
  72.1 0.0 all-gather.8.cloned.1.call-update
  72.2 0.0 reduce-scatter.5.cloned.1.call-start
  72.2 0.9 select_reduce_fusion
  73.1 0.1 reshape.151
  73.2 0.9 convert_log_fusion
  74.2 0.1 constant_dynamic-slice_fusion
  74.2 0.7 gather_fusion.1
  75.0 17.3 %all-gather.10.cloned.1.call-done = bf16[1024,512]{1,0:T(8,128)(2,1)} async-done(((bf16[1024,256]{1,0:T(8,128)(2,1)}), bf16[1024,512]{1,0:T(8,128)(2,1)}) %all-gather.10.cloned.1.call-update) | async-done | bytes 1048592 | tf_op jit(solution)/shard_map/all_gather | solution.py:50
  92.3 22.9 %all-gather.12.cloned.1.call-done = bf16[1024,512]{1,0:T(8,128)(2,1)} async-done(((bf16[1024,256]{1,0:T(8,128)(2,1)}), bf16[1024,512]{1,0:T(8,128)(2,1)}) %all-gather.12.cloned.1.call-update) | async-done | bytes 1048592 | tf_op jit(solution)/shard_map/all_gather | solution.py:51
  115.3 1.9 multiply_reduce_fusion
  117.1 127.3 %all-gather.8.cloned.1.call-done = bf16[16384,512]{1,0:T(8,128)(2,1)} async-done(((bf16[1024,512]{1,0:T(8,128)(2,1)}), bf16[16384,512]{1,0:T(8,128)(2,1)}) %all-gather.8.cloned.1.call-update) | async-done | bytes 16777232 | tf_op jit(solution)/shard_map/all_gather | solution.py:61
  244.4 0.0 copy-start.3
  244.4 19.7 %gather_fusion = bf16[256,128,512]{2,1,0:T(8,128)(2,1)} fusion(bf16[128,128,512]{2,1,0:T(8,128)(2,1)} %bitcast.94, s32[1024]{0:T(1024)S(1)} %pad_clamp_fusion), kind=kCustom, calls=%fused_computation | custom fusion | bytes 67109888 | tf_op jit(solution)/shard_map/gather | solution.py:64
  264.2 0.0 copy-done.3
  264.2 28.0 %bitcast_reduce_fusion = (f32[4,256]{1,0:T(4,128)S(1)}, f32[4,8192,256]{2,1,0:T(8,128)}) fusion(f32[4,8192]{1,0:T(4,128)S(1)} %sub.107, bf16[4,8192,512]{2,1,0:T(8,128)(2,1)} %bitcast.95, bf16[4,256,512]{2,1,0:T(8,128)(2,1)S(1)} %bitcast.100), kind=kOutput, calls=%fused_computation.4 | convolution fusion | flops 8615099392 | bytes 68292608 | tf_op jit(solution)/shard_map/gqe,gke->gqk/dot_general | solution.py:68
  292.2 14.3 %fusion.1 = f32[4,256]{1,0:T(4,128)S(1)} fusion(f32[4,8192,256]{2,1,0:T(8,128)} %get-tuple-element.25, f32[4,256]{1,0:T(4,128)S(1)} %get-tuple-element.24, f32[4,8192]{1,0:T(4,128)S(1)} %sub.107), kind=kLoop, calls=%fused_computation.6 | loop fusion | flops 33553408 | bytes 33693696 | tf_op jit(solution)/shard_map/reduce_sum | solution.py:72
  306.5 4.3 %all-gather.3 = f32[2,4,256]{2,1,0:T(4,128)S(1)} all-gather(f32[1,4,256]{2,1,0:T(4,128)S(1)} %bitcast.104), channel_id=3, replica_groups=mesh['cat'=16,'tp'=2] {'tp'}, dimensions={0}, use_global_device_ids=true | all-gather | bytes 12288 | tf_op jit(solution)/shard_map/all_gather | solution.py:12
  310.8 4.3 %all-gather.2 = f32[2,4,256]{2,1,0:T(4,128)S(1)} all-gather(f32[1,4,256]{2,1,0:T(4,128)S(1)} %bitcast.103), channel_id=2, replica_groups=mesh['cat'=16,'tp'=2] {'tp'}, dimensions={0}, use_global_device_ids=true | all-gather | bytes 12288 | tf_op jit(solution)/shard_map/all_gather | solution.py:12
  315.2 0.6 exponential_add_fusion
  315.8 0.0 copy-start.2
  315.8 0.0 copy-start.1
  315.9 24.3 %fusion.9 = bf16[4,256,512]{2,1,0:T(8,128)(2,1)} fusion(bf16[4,8192,512]{2,1,0:T(8,128)(2,1)} %bitcast.96, f32[4,8192,256]{2,1,0:T(8,128)} %get-tuple-element.25, f32[4,256]{1,0:T(4,128)S(1)} %fusion.16, f32[4,8192]{1,0:T(4,128)S(1)} %sub.107), kind=kOutput, calls=%fused_computation.15 | convolution fusion | flops 8624013312 | bytes 68292608 | tf_op jit(solution)/shard_map/gqk,gke->gqe/dot_general | solution.py:79
  340.1 0.0 reduce-scatter.5.cloned.1.call-update
  340.1 18.6 %reduce-scatter.5.cloned.1.call-done = bf16[1024,256]{1,0:T(8,128)(2,1)} async-done(((bf16[1024,512]{1,0:T(8,128)(2,1)}), bf16[1024,256]{1,0:T(8,128)(2,1)}) %reduce-scatter.5.cloned.1.call-update) | async-done | bytes 524304 | tf_op jit(solution)/shard_map/reduce_scatter | solution.py:81
  358.8 0.0 copy-done.2
  358.8 2.1 multiply_convert_fusion
  360.9 0.0 copy-done.1
  (11 shorter events, 0.1 us)
Async XLA Ops:
  7.2 1.9 copy-start
  7.2 62.3 %reduce-scatter.3.cloned.1.call-start = ((), (), s32[]{:S(2)}) async-start(), calls=%async_computation.2 | async-start | bytes 6291456 | tf_op jit(solution)/shard_map/reduce_scatter | solution.py:40
  12.3 80.0 %all-gather.10.cloned.1.call-start = ((), (), s32[]{:S(2)}) async-start(), calls=%async_computation.4 | async-start | bytes 1572864 | tf_op jit(solution)/shard_map/all_gather | solution.py:50
  13.0 102.2 %all-gather.12.cloned.1.call-start = ((), (), s32[]{:S(2)}) async-start(), calls=%async_computation.5 | async-start | bytes 1572864 | tf_op jit(solution)/shard_map/all_gather | solution.py:51
  13.8 230.7 %all-gather.8.cloned.1.call-start = ((), (), s32[]{:S(2)}) async-start(), calls=%async_computation.3 | async-start | bytes 17825792 | tf_op jit(solution)/shard_map/all_gather | solution.py:61
  72.2 286.6 %reduce-scatter.5.cloned.1.call-start = ((), (), s32[]{:S(2)}) async-start(), calls=%async_computation.6 | async-start | bytes 1572864 | tf_op jit(solution)/shard_map/reduce_scatter | solution.py:81
  244.4 19.7 %copy-start.3 = (bf16[1024,512]{1,0:T(8,128)(2,1)S(1)}, bf16[1024,512]{1,0:T(8,128)(2,1)}, u32[]{:S(2)}) copy-start(bf16[1024,512]{1,0:T(8,128)(2,1)} %all-gather.10.cloned.1.call-done) | copy-start | bytes 3145732
  315.8 42.9 %copy-start.2 = (bf16[1024,256]{1,0:T(8,128)(2,1)S(1)}, bf16[1024,256]{1,0:T(8,128)(2,1)}, u32[]{:S(2)}) copy-start(bf16[1024,256]{1,0:T(8,128)(2,1)} %param.8) | copy-start | bytes 1572868
  315.8 45.1 %copy-start.1 = (bf16[512,512]{1,0:T(8,128)(2,1)S(1)}, bf16[512,512]{1,0:T(8,128)(2,1)}, u32[]{:S(2)}) copy-start(bf16[512,512]{1,0:T(8,128)(2,1)} %param.10) | copy-start | bytes 1572868
Sparse Core Ops, SparseCore 0:
  12.4 56.9 reduce-scatter.2
  71.0 21.2 all-gather.9
  94.0 21.2 all-gather.11
  117.5 126.8 all-gather.7
  340.3 18.4 reduce-scatter.4
where the time goes:
time: 368 us; the launch traced here: 367 us
  waiting for transfers between devices  243 us (66%)
  matrix products  55.5 us (15%)
  other arithmetic  23.5 us (6%)
  local copies, waits for them, and re-layouts  22.5 us (6%)
  between operations  13.9 us (4%)
  blocking collectives  8.67 us (2%)
    all_gather x1, waiting for transfers between devices, local(): lax.all_gather(item_vec, 'cat', axis=0, tiled=True)  127 us
    reduce_scatter x1, waiting for transfers between devices, local(): lax.psum_scatter(jnp.dot(reordered, item_weight, preferred_element_type=j...  55.6 us
    dot_general x1, matrix products, local(): jnp.einsum('gqe,gke->gqk', query_rows, picked, preferred_element_type=jnp...  28 us
    dot_general x1, matrix products, local(): jnp.einsum('gqk,gke->gqe', weights, picked, preferred_element_type=jnp.fl...  24.3 us
    all_gather x1, waiting for transfers between devices, local(): lax.all_gather(positive_emb, 'tp', axis=1, tiled=True)  22.9 us
    gather x1, local copies, waits for them, and re-layouts, local(): picked = item_table[home_ids].reshape(qblock_count, -1, feat_width)  19.7 us
    reduce_scatter x1, waiting for transfers between devices, local(): lax.psum_scatter(flat_sum.astype(jnp.bfloat16), 'tp', scatter_dimension=1...  18.6 us
    all_gather x1, waiting for transfers between devices, local(): lax.all_gather(query_emb, 'tp', axis=1, tiled=True)  17.3 us
  transfers between devices with their start and end apart: 5, of which 5 were waited for; matrix products, arithmetic and copies ran while one was open for 2% of the time, Pallas kernels for 0%

commit v1 on v0

v1 whole, which is shorter than its diff:
```python
import functools
import math

import jax
import jax.numpy as jnp
from jax import lax
from jax.experimental import pallas as pl
from jax.experimental.pallas import tpu as pltpu
from jax.sharding import PartitionSpec as P

BLK = 256
LANES = 128
CHUNKS = 2
NEG = -1e30
LOG2E = math.log2(math.e)
LN2 = math.log(2.0)


def lookup(index, values):
    result = values[0]
    for place, value in enumerate(values[1:], 1):
        result = jnp.where(index == place, value, result)
    return result


def nearest(count):
    return [sorted(range(count), key=lambda other: abs(other - at)) for at in range(count)]


def kernel(
    sizes, scale,
    q_ref, pos_ref, h_ref, w_ref, bias_ref, loss_ref, grad_ref,
    table, hbuf, wbuf, qbuf, qfull, run_max, run_sum, acc, osend, orecv, stats,
    local_sem, w_send, w_recv, q_send, q_recv, h_send, h_recv,
    t_send, t_recv, o_send, o_recv, s_send, s_recv,
):
    tp, rows_a, rows_b = sizes
    me_t = lax.axis_index("tp")
    me_c = lax.axis_index("cat")
    core = me_c % 2
    at_b = (me_c // 2) % rows_b
    at_a = me_c // (2 * rows_b)
    queries, width = q_ref.shape
    feats = table.shape[2]
    chunk_rows = table.shape[1]
    own_blocks, _, _ = h_ref.shape
    sub_rows = BLK // tp
    groups = queries // BLK
    part_blocks = own_blocks // CHUNKS

    def cat_of(a, b, k):
        return (a * rows_b + b) * 2 + k

    ways = [
        (at_a > 0, cat_of(at_a - 1, at_b, core)),
        (at_a < rows_a - 1, cat_of(at_a + 1, at_b, core)),
        (at_b > 0, cat_of(at_a, at_b - 1, core)),
        (at_b < rows_b - 1, cat_of(at_a, at_b + 1, core)),
        (at_a >= 0, cat_of(at_a, at_b, 1 - core)),
    ]
    peers = [lax.rem(me_t + d, tp) for d in range(1, tp)]

    barrier = pltpu.get_barrier_semaphore()
    total = jnp.int32(tp - 1)
    for peer in peers:
        pl.semaphore_signal(barrier, inc=1, device_id={"tp": peer}, device_id_type=pl.DeviceIdType.MESH)
    for there, target in ways:
        @pl.when(there)
        def _():
            pl.semaphore_signal(barrier, inc=1, device_id={"cat": target}, device_id_type=pl.DeviceIdType.MESH)
        total = total + there.astype(jnp.int32)
    pl.semaphore_wait(barrier, total)

    def across(src, dst, send, recv, peer):
        return pltpu.make_async_remote_copy(
            src_ref=src, dst_ref=dst, send_sem=send, recv_sem=recv,
            device_id={"tp": peer}, device_id_type=pl.DeviceIdType.MESH,
        )

    def w_copy(slot, d, peer):
        return across(w_ref, wbuf.at[slot], w_send.at[d], w_recv.at[slot], peer)

    def q_copy(slot, d, peer):
        return across(q_ref, qbuf.at[slot], q_send.at[d], q_recv.at[slot], peer)

    def h_part(part, owner):
        return h_ref.at[
            pl.ds(part * part_blocks, part_blocks),
            pl.ds(pl.multiple_of(owner * sub_rows, sub_rows), sub_rows),
        ]

    def h_copy(slot, d, part, peer):
        return across(h_part(part, peer), hbuf.at[slot, part], h_send.at[d, part], h_recv.at[slot, part], peer)

    for d, peer in enumerate(peers):
        w_copy(me_t, d, peer).start()
    for part in range(CHUNKS):
        for d, peer in enumerate(peers):
            h_copy(me_t, d, part, peer).start()
    for d, peer in enumerate(peers):
        q_copy(me_t, d, peer).start()
    own = [
        pltpu.make_async_copy(w_ref, wbuf.at[me_t], local_sem.at[0]),
        pltpu.make_async_copy(q_ref, qbuf.at[me_t], local_sem.at[1]),
    ] + [
        pltpu.make_async_copy(h_part(part, me_t), hbuf.at[me_t, part], local_sem.at[2 + part])
        for part in range(CHUNKS)
    ]
    for copy in own:
        copy.start()

    run_max[...] = jnp.full_like(run_max, NEG)
    run_sum[...] = jnp.zeros_like(run_sum)
    acc[...] = jnp.zeros_like(acc)
    diag = lax.broadcasted_iota(jnp.int32, (LANES, LANES), 0) == lax.broadcasted_iota(
        jnp.int32, (LANES, LANES), 1
    )
    stat_rows = queries // LANES

    def as_row(column):
        return jnp.sum(jnp.where(diag, column, 0.0), axis=0, keepdims=True)

    def as_column(row):
        return jnp.sum(jnp.where(diag, row, 0.0), axis=1, keepdims=True)

    def table_copy(slot, way):
        return pltpu.make_async_remote_copy(
            src_ref=table.at[slot], dst_ref=table.at[slot],
            send_sem=t_send.at[slot, way], recv_sem=t_recv.at[slot],
            device_id={"cat": ways[way][1]}, device_id_type=pl.DeviceIdType.MESH,
        )

    def sends(a, b):
        return [
            ways[0][0] & (b == at_b) & (a >= at_a),
            ways[1][0] & (b == at_b) & (a <= at_a),
            ways[2][0] & (b >= at_b),
            ways[3][0] & (b <= at_b),
            ways[4][0],
        ]

    def hand_on(a, b, part, act):
        slot = cat_of(a, b, core) * CHUNKS + part
        for way, wanted in enumerate(sends(a, b)):
            @pl.when(wanted)
            def _():
                act(table_copy(slot, way))

    own[0].wait()
    for d, peer in enumerate(peers):
        w_copy(peer, d, peer).wait_recv()
    for part in range(CHUNKS):
        own[2 + part].wait()
        for d, peer in enumerate(peers):
            h_copy(peer, d, part, peer).wait_recv()
        vec = jnp.zeros((chunk_rows, feats), jnp.float32)
        for t in range(tp):
            vec = vec + jnp.dot(
                hbuf[t, part].reshape(chunk_rows, hbuf.shape[-1]), wbuf[t],
                preferred_element_type=jnp.float32,
            )
        table[me_c * CHUNKS + part] = vec.astype(jnp.bfloat16)
        hand_on(at_a, at_b, part, lambda copy: copy.start())

    own[1].wait()
    for d, peer in enumerate(peers):
        q_copy(peer, d, peer).wait_recv()
    for t in range(tp):
        qfull[:, t * width:(t + 1) * width] = qbuf[t]
    for row in range(stat_rows):
        rows = slice(row * LANES, (row + 1) * LANES)
        product = qbuf[me_t, rows, :].astype(jnp.float32) * pos_ref[rows, :].astype(jnp.float32)
        stats[me_t, stat_rows + row:stat_rows + row + 1, :] = as_row(
            jnp.sum(product, axis=1, keepdims=True)
        )

    def attend(slot):
        items = table[slot]
        for g in range(groups):
            rows = slice(g * BLK, (g + 1) * BLK)
            raw = lax.dot_general(
                qfull[rows, :], items, (((1,), (1,)), ((), ())), preferred_element_type=jnp.float32
            )
            tiles = [
                raw[:, i * LANES:(i + 1) * LANES] * (scale * LOG2E) + bias_ref[g, slot, i:i + 1, :]
                for i in range(chunk_rows // LANES)
            ]
            top = functools.reduce(jnp.maximum, tiles)
            old_max = run_max[rows, :]
            new_max = jnp.maximum(old_max, jnp.max(top, axis=1, keepdims=True))
            fade = jnp.exp2(old_max - new_max)
            tiles = [jnp.exp2(tile - new_max) for tile in tiles]
            run_max[rows, :] = new_max
            run_sum[rows, :] = run_sum[rows, :] * fade + functools.reduce(jnp.add, tiles)
            weights = jnp.concatenate([tile.astype(jnp.bfloat16) for tile in tiles], axis=1)
            part = jnp.dot(weights, items, preferred_element_type=jnp.float32)
            for i in range(feats // LANES):
                cols = slice(i * LANES, (i + 1) * LANES)
                acc[rows, cols] = acc[rows, cols] * fade + part[:, cols]

    ranks = sorted(
        [(i, j) for i in range(rows_a) for j in range(rows_b)], key=lambda r: (r[0] + r[1], r[1])
    )
    near_a, near_b = nearest(rows_a), nearest(rows_b)

    def source(index):
        rank_a = lookup(index, [r[0] for r in ranks])
        rank_b = lookup(index, [r[1] for r in ranks])
        a = lookup(rank_a * rows_a + at_a, [near_a[p][r] for r in range(rows_a) for p in range(rows_a)])
        b = lookup(rank_b * rows_b + at_b, [near_b[p][r] for r in range(rows_b) for p in range(rows_b)])
        return a, b

    @pl.loop(0, len(ranks) * CHUNKS)
    def _(step):
        index, part = step // CHUNKS, step % CHUNKS
        a, b = source(index)

        @pl.when(index > 0)
        def _():
            table_copy(cat_of(a, b, core) * CHUNKS + part, 4).wait_recv()
            hand_on(a, b, part, lambda copy: copy.start())

        @pl.loop(0, 2)
        def _(other):
            slot = cat_of(a, b, (core + other) % 2) * CHUNKS + part

            @pl.when(other > 0)
            def _():
                table_copy(slot, 4).wait_recv()

            attend(slot)

    def o_copy(slot, d, g, peer):
        rows = pl.ds(g * BLK, BLK)
        return across(osend.at[d, rows], orecv.at[slot, rows], o_send.at[d, g], o_recv.at[slot, g], peer)

    def s_copy(slot, d, peer):
        return across(stats.at[slot], stats.at[slot], s_send.at[d], s_recv.at[slot], peer)

    for g in range(groups):
        rows = slice(g * BLK, (g + 1) * BLK)
        norm = jnp.sum(run_sum[rows, :], axis=1, keepdims=True)
        lse = run_max[rows, 0:1] + jnp.log2(norm)
        inverse = 1.0 / norm
        for i in range(BLK // LANES):
            row = g * (BLK // LANES) + i
            stats[me_t, row:row + 1, :] = as_row(lse[i * LANES:(i + 1) * LANES, :])
        for d, peer in enumerate(peers):
            cols = pl.ds(pl.multiple_of(peer * width, LANES), width)
            osend[d, rows, :] = (acc[rows, cols] * inverse).astype(jnp.bfloat16)
            o_copy(me_t, d, g, peer).start()
        cols = pl.ds(pl.multiple_of(me_t * width, LANES), width)
        acc[rows, cols] = acc[rows, cols] * inverse
    for d, peer in enumerate(peers):
        s_copy(me_t, d, peer).start()
    for d, peer in enumerate(peers):
        s_copy(peer, d, peer).wait_recv()
    for g in range(groups):
        for d, peer in enumerate(peers):
            o_copy(peer, d, g, peer).wait_recv()
        for i in range(BLK // LANES):
            row = g * (BLK // LANES) + i
            rows = slice(row * LANES, (row + 1) * LANES)
            pos = sum(stats[t, stat_rows + row:stat_rows + row + 1, :] for t in range(tp)) * (scale * LOG2E)
            lses = [stats[t, row:row + 1, :] for t in range(tp)]
            top = functools.reduce(jnp.maximum, lses + [pos])
            log_total = top + jnp.log2(sum(jnp.exp2(v - top) for v in lses + [pos]))
            loss_ref[row:row + 1, :] = (log_total - pos) * LN2
            shift = as_column(log_total)
            cols = pl.ds(pl.multiple_of(me_t * width, LANES), width)
            grad = acc[rows, cols] * jnp.exp2(as_column(stats[me_t, row:row + 1, :]) - shift)
            for peer in peers:
                share = jnp.exp2(as_column(stats[peer, row:row + 1, :]) - shift)
                grad = grad + orecv[peer, rows, :].astype(jnp.float32) * share
            pos_weight = jnp.exp2(as_column(pos - log_total)) - 1.0
            grad = grad + pos_weight * pos_ref[rows, :].astype(jnp.float32)
            grad_ref[rows, :] = (scale * grad).astype(jnp.bfloat16)

    for d, peer in enumerate(peers):
        w_copy(me_t, d, peer).wait_send()
        q_copy(me_t, d, peer).wait_send()
        for part in range(CHUNKS):
            h_copy(me_t, d, part, peer).wait_send()
        for g in range(groups):
            o_copy(me_t, d, g, peer).wait_send()
        s_copy(me_t, d, peer).wait_send()

    @pl.loop(0, len(ranks) * CHUNKS)
    def _(step):
        index, part = step // CHUNKS, step % CHUNKS
        a, b = source(index)
        hand_on(a, b, part, lambda copy: copy.wait_send())


def local(query_emb, positive_emb, item_hidden, item_weight, neg_blocks, block_home, sample_counts):
    tp = lax.axis_size("tp")
    cats = lax.axis_size("cat")
    rows_a = 4
    rows_b = cats // 2 // rows_a
    me_t = lax.axis_index("tp")
    queries, width = query_emb.shape
    hid, feats = item_weight.shape
    own_blocks = item_hidden.shape[0] // BLK
    sub_rows = BLK // tp
    total_blocks = block_home.shape[0]
    groups = neg_blocks.shape[0]
    chunk_rows = own_blocks * sub_rows // CHUNKS
    slots = cats * CHUNKS
    scale = 2.0 / math.sqrt(feats)

    ids = jnp.arange(total_blocks, dtype=jnp.int32)
    chosen = jnp.any(neg_blocks[:, :, None] == ids, axis=1)
    stored = jnp.any(chosen[:, :, None] & (block_home[:, None] == ids), axis=1)
    log_q = jnp.log(sample_counts.astype(jnp.float32)).reshape(total_blocks, tp, sub_rows)
    log_q = lax.dynamic_index_in_dim(log_q, me_t, 1, keepdims=False)
    bias = jnp.where(stored[:, :, None], log_q * -LOG2E, NEG).reshape(
        groups, slots, chunk_rows // LANES, LANES
    )
    vmem = pl.BlockSpec(memory_space=pltpu.VMEM)
    hbm = pl.BlockSpec(memory_space=pl.ANY)
    dma = pltpu.SemaphoreType.DMA
    others = max(tp - 1, 1)
    flops = 4 * queries * slots * chunk_rows * feats
    loss, grad = pl.pallas_call(
        functools.partial(kernel, (tp, rows_a, rows_b), scale),
        out_shape=(
            jax.ShapeDtypeStruct((queries // LANES, LANES), jnp.float32),
            jax.ShapeDtypeStruct((queries, width), jnp.bfloat16),
        ),
        in_specs=[hbm, vmem, hbm, hbm, vmem],
        out_specs=(vmem, vmem),
        scratch_shapes=[
            pltpu.VMEM((slots, chunk_rows, feats), jnp.bfloat16),
            pltpu.VMEM((tp, CHUNKS, own_blocks // CHUNKS, sub_rows, hid), jnp.bfloat16),
            pltpu.VMEM((tp, hid, feats), jnp.bfloat16),
            pltpu.VMEM((tp, queries, width), jnp.bfloat16),
            pltpu.VMEM((queries, feats), jnp.bfloat16),
            pltpu.VMEM((queries, LANES), jnp.float32),
            pltpu.VMEM((queries, LANES), jnp.float32),
            pltpu.VMEM((queries, feats), jnp.float32),
            pltpu.VMEM((others, queries, width), jnp.bfloat16),
            pltpu.VMEM((tp, queries, width), jnp.bfloat16),
            pltpu.VMEM((tp, 2 * queries // LANES, LANES), jnp.float32),
            dma((2 + CHUNKS,)),
            dma((others,)), dma((tp,)),
            dma((others,)), dma((tp,)),
            dma((others, CHUNKS)), dma((tp, CHUNKS)),
            dma((slots, 5)), dma((slots,)),
            dma((others, groups)), dma((tp, groups)),
            dma((others,)), dma((tp,)),
        ],
        compiler_params=pltpu.CompilerParams(
            collective_id=0, has_side_effects=True, vmem_limit_bytes=48 * 1024 * 1024
        ),
        cost_estimate=pl.CostEstimate(
            flops=flops, bytes_accessed=8 * 1024 * 1024, transcendentals=queries * slots * chunk_rows
        ),
    )(
        query_emb, positive_emb, item_hidden.reshape(own_blocks, BLK, hid), item_weight, bias,
    )
    return loss.reshape(-1), grad


def solution(mesh):
    placed = (
        P("cat", "tp"),
        P("cat", "tp"),
        P("cat", "tp"),
        P("tp", None),
        P("cat", None),
        P(),
        P(),
    )
    return jax.shard_map(
        local, mesh=mesh, in_specs=placed, out_specs=(P("cat"), P("cat", "tp")), check_vma=False
    )
```

time: 368 us -> 169 us (0.46)
  waiting for transfers between devices: 243 us -> 0 us
  Pallas kernels: 0 us -> 158 us
  matrix products: 55.5 us -> 0 us
  other arithmetic: 23.5 us -> 2.91 us
  local copies, waits for them, and re-layouts: 22.5 us -> 6.23 us
  between operations: 13.9 us -> 0.69 us
  blocking collectives: 8.67 us -> 0 us
    all_gather x3 -> x0, waiting for transfers between devices: 168 us -> none  [the longest x1 127 us: local(): lax.all_gather(item_vec, 'cat', axis=0, tiled=True)]
    pallas_call x0 -> x1, Pallas kernels: none -> 158 us  [local(): pl.pallas_call(functools.partial(kernel, (tp, rows_a, rows_b), scale), ou...]
    reduce_scatter x2 -> x0, waiting for transfers between devices: 74.2 us -> none  [the longest x1 55.6 us: local(): lax.psum_scatter(jnp.dot(reordered, item_weight, preferred_element_type=j...]
    dot_general x3 -> x0, matrix products: 55.5 us -> none  [the longest x1 28 us: local(): jnp.einsum('gqe,gke->gqk', query_rows, picked, preferred_element_type=jnp...]
    gather x2 -> x0, local copies, waits for them, and re-layouts: 20.4 us -> none  [the longest x1 19.7 us: local(): picked = item_table[home_ids].reshape(qblock_count, -1, feat_width)]
    reduce_sum x3 -> x0, other arithmetic: 17.1 us -> none  [the longest x1 14.3 us: local(): run_sum = jnp.sum(jnp.exp(scores - run_max[..., None]), axis=2)]
    all_gather x2 -> x0, blocking collectives: 8.67 us -> none  [merged(): pieces = jax.tree.map(lambda part: lax.all_gather(part, axis), value)]
    unnamed x14 -> x10, local copies, waits for them, and re-layouts: 0.05 us -> 6.1 us
  transfers between devices with their start and end apart: 5 -> 0, of which waited for: 5 -> 0; matrix products, arithmetic and copies ran while one was open for 2% -> 0% of each run, Pallas kernels for 0% -> 0%
where the time goes in v1:
time: 169 us; the launch traced here: 168 us
  Pallas kernels  158 us (93%)
  local copies, waits for them, and re-layouts  6.23 us (4%)
  other arithmetic  2.91 us (2%)
    pallas_call x1, Pallas kernels, local(): pl.pallas_call(functools.partial(kernel, (tp, rows_a, rows_b), scale), ou...  158 us
    unnamed x10, local copies, waits for them, and re-layouts  6.1 us

profile of v1, /device:TPU:0, one launch (start us, length us, event | category | flops | bytes accessed | tf_op | source)
XLA Modules:
  0.0 168.2 jit_solution(10766956645936887309)
XLA Ops:
  0.6 0.8 fusion
  1.4 0.7 iota_compare_fusion.1
  2.2 0.1 and_reduce_fusion
  2.3 0.1 broadcast_in_dim.25
  2.5 0.9 convert_log_fusion
  3.4 0.1 dynamic-slice_multiply_fusion
  3.5 0.2 broadcast_select_fusion.bias_ref
  3.7 0.0 copy-start
  3.7 1.6 copy-done
  5.3 0.0 copy-start.1
  5.3 1.0 copy-done.1
  6.3 0.0 copy-start.2
  6.3 1.0 copy-done.2
  7.4 0.0 copy-start.3
  7.4 1.0 copy-done.3
  8.4 158.4 %shard_map.86 = (f32[8,128]{1,0:T(8,128)S(1)}, bf16[1024,256]{1,0:T(8,128)(2,1)S(1)}) custom-call(bf16[1024,256]{1,0:T(8,128)(2,1)S(1)} %copy-done.1, bf16[1024,256]{1,0:T(8,128)(2,1)S(1)} %copy-done.2, bf16[8,256,512]{2,1,0:T(8,128)(2,1)S(1)} %bitcast.5, bf16[512,512]{1,0:T(8,128)(2,1)S(1)} %copy-done.3, f32[4,32,4,128]{3,2,1,0:T(4,128)S(1)} %broadcast_select_fusion.bias_ref), custom_call_target="tpu_custom_call" | custom-call | flops 34359738368 | bytes 8388608 | tf_op jit(solution)/shard_map/pallas_call | solution.py:324
  166.9 0.6 copy.11
  167.5 0.8 copy.12
Async XLA Ops:
  3.7 1.6 copy-start
  5.3 1.0 copy-start.1
  6.3 1.0 copy-start.2
  7.4 1.0 copy-start.3

commit v2 on v1

--- a/solution.py
+++ b/solution.py
@@ -10,7 +10,8 @@
 
 BLK = 256
 LANES = 128
-CHUNKS = 2
+CHUNKS = 4
+AHEAD = 3
 NEG = -1e30
 LOG2E = math.log2(math.e)
 LN2 = math.log(2.0)
@@ -29,9 +30,9 @@
 
 def kernel(
     sizes, scale,
-    q_ref, pos_ref, h_ref, w_ref, bias_ref, loss_ref, grad_ref,
-    table, hbuf, wbuf, qbuf, qfull, run_max, run_sum, acc, osend, orecv, stats,
-    local_sem, w_send, w_recv, q_send, q_recv, h_send, h_recv,
+    q_ref, pos_in, h_ref, w_ref, bias_ref, loss_ref, grad_ref,
+    table, hbuf, wbuf, qbuf, pos_ref, qfull, run_max, run_sum, acc, osend, orecv, stats,
+    local_sem, w_send, w_recv, w_pass, q_send, q_recv, h_send, h_recv,
     t_send, t_recv, o_send, o_recv, s_send, s_recv,
 ):
     tp, rows_a, rows_b = sizes
@@ -41,12 +42,13 @@
     at_b = (me_c // 2) % rows_b
     at_a = me_c // (2 * rows_b)
     queries, width = q_ref.shape
-    feats = table.shape[2]
-    chunk_rows = table.shape[1]
+    feats = table.shape[3]
+    chunk_rows = table.shape[2]
     own_blocks, _, _ = h_ref.shape
     sub_rows = BLK // tp
     groups = queries // BLK
     part_blocks = own_blocks // CHUNKS
+    half = wbuf.shape[2]
 
     def cat_of(a, b, k):
         return (a * rows_b + b) * 2 + k
@@ -77,8 +79,18 @@
             device_id={"tp": peer}, device_id_type=pl.DeviceIdType.MESH,
         )
 
+    def w_half(k):
+        return w_ref.at[pl.ds(pl.multiple_of(k * half, half), half)]
+
     def w_copy(slot, d, peer):
-        return across(w_ref, wbuf.at[slot], w_send.at[d], w_recv.at[slot], peer)
+        return across(w_half(core), wbuf.at[slot, core], w_send.at[d], w_recv.at[slot, core], peer)
+
+    def w_hand(slot, k, d):
+        return pltpu.make_async_remote_copy(
+            src_ref=wbuf.at[slot, k], dst_ref=wbuf.at[slot, k],
+            send_sem=w_pass.at[d], recv_sem=w_recv.at[slot, k],
+            device_id={"cat": ways[4][1]}, device_id_type=pl.DeviceIdType.MESH,
+        )
 
     def q_copy(slot, d, peer):
         return across(q_ref, qbuf.at[slot], q_send.at[d], q_recv.at[slot], peer)
@@ -94,19 +106,18 @@
 
     for d, peer in enumerate(peers):
         w_copy(me_t, d, peer).start()
-    for part in range(CHUNKS):
-        for d, peer in enumerate(peers):
-            h_copy(me_t, d, part, peer).start()
-    for d, peer in enumerate(peers):
-        q_copy(me_t, d, peer).start()
+        h_copy(me_t, d, 0, peer).start()
     own = [
-        pltpu.make_async_copy(w_ref, wbuf.at[me_t], local_sem.at[0]),
-        pltpu.make_async_copy(q_ref, qbuf.at[me_t], local_sem.at[1]),
-    ] + [
-        pltpu.make_async_copy(h_part(part, me_t), hbuf.at[me_t, part], local_sem.at[2 + part])
-        for part in range(CHUNKS)
+        pltpu.make_async_copy(w_half(0), wbuf.at[me_t, 0], local_sem.at[0]),
+        pltpu.make_async_copy(w_half(1), wbuf.at[me_t, 1], local_sem.at[1]),
+        pltpu.make_async_copy(q_ref, qbuf.at[me_t], local_sem.at[2]),
+        pltpu.make_async_copy(pos_in, pos_ref, local_sem.at[3]),
     ]
-    for copy in own:
+
+    def own_part(part):
+        return pltpu.make_async_copy(h_part(part, me_t), hbuf.at[me_t, part], local_sem.at[4 + part])
+
+    for copy in own + [own_part(part) for part in range(CHUNKS)]:
         copy.start()
 
     run_max[...] = jnp.full_like(run_max, NEG)
@@ -123,67 +134,113 @@
     def as_column(row):
         return jnp.sum(jnp.where(diag, row, 0.0), axis=1, keepdims=True)
 
-    def table_copy(slot, way):
+    def pair_of(a, b, part):
+        return (a * rows_b + b) * CHUNKS + part
+
+    def table_copy(pair, k, way):
         return pltpu.make_async_remote_copy(
-            src_ref=table.at[slot], dst_ref=table.at[slot],
-            send_sem=t_send.at[slot, way], recv_sem=t_recv.at[slot],
+            src_ref=table.at[pair, k], dst_ref=table.at[pair, k],
+            send_sem=t_send.at[pair, way], recv_sem=t_recv.at[pair, k],
             device_id={"cat": ways[way][1]}, device_id_type=pl.DeviceIdType.MESH,
         )
 
-    def sends(a, b):
+    def sends(a, b, part):
+        b_first = (part == 2) & (a != rows_a // 2)
+        along_a = b_first | (b == at_b)
+        along_b = jnp.logical_not(b_first) | (a == at_a)
         return [
-            ways[0][0] & (b == at_b) & (a >= at_a),
-            ways[1][0] & (b == at_b) & (a <= at_a),
-            ways[2][0] & (b >= at_b),
-            ways[3][0] & (b <= at_b),
+            ways[0][0] & along_a & (a >= at_a),
+            ways[1][0] & along_a & (a <= at_a),
+            ways[2][0] & along_b & (b >= at_b),
+            ways[3][0] & along_b & (b <= at_b),
             ways[4][0],
         ]
 
     def hand_on(a, b, part, act):
-        slot = cat_of(a, b, core) * CHUNKS + part
-        for way, wanted in enumerate(sends(a, b)):
+        pair = pair_of(a, b, part)
+        for way, wanted in enumerate(sends(a, b, part)):
             @pl.when(wanted)
             def _():
-                act(table_copy(slot, way))
+                act(table_copy(pair, core, way))
+
+    order = sorted(
+        [(i, j, p) for p in range(CHUNKS) for i in range(rows_a) for j in range(rows_b)],
+        key=lambda r: (r[0] + r[1] + (rows_a - 0.5) * r[2], r[1]),
+    )
+    near_a, near_b = nearest(rows_a), nearest(rows_b)
+
+    def source(step):
+        rank_a, rank_b, part = (lookup(step, [r[i] for r in order]) for i in range(3))
+        a = lookup(rank_a * rows_a + at_a, [near_a[p][r] for r in range(rows_a) for p in range(rows_a)])
+        b = lookup(rank_b * rows_b + at_b, [near_b[p][r] for r in range(rows_b) for p in range(rows_b)])
+        return a, b, part
+
+    def advance(step):
+        a, b, part = source(step)
+        mine = (a == at_a) & (b == at_b)
+
+        @pl.when(mine)
+        def _():
+            own_part(part).wait()
+            for d, peer in enumerate(peers):
+                h_copy(peer, d, part, peer).wait_recv()
+            vec = jnp.zeros((chunk_rows, feats), jnp.float32)
+            for t in range(tp):
+                for k in range(2):
+                    hidden = hbuf[t, part, :, :, k * half:(k + 1) * half]
+                    vec = vec + jnp.dot(
+                        hidden.reshape(chunk_rows, half), wbuf[t, k], preferred_element_type=jnp.float32
+                    )
+            table[pair_of(a, b, part), core] = vec.astype(jnp.bfloat16)
+
+        @pl.when(jnp.logical_not(mine))
+        def _():
+            table_copy(pair_of(a, b, part), core, 4).wait_recv()
+
+        hand_on(a, b, part, lambda copy: copy.start())
+
+    def partner(step):
+        pair = pair_of(*source(step))
+        table_copy(pair, 1 - core, 4).wait_recv()
+        return pair
 
     own[0].wait()
+    own[1].wait()
     for d, peer in enumerate(peers):
         w_copy(peer, d, peer).wait_recv()
-    for part in range(CHUNKS):
-        own[2 + part].wait()
+        w_hand(peer, core, d).start()
+    for d, peer in enumerate(peers):
+        w_hand(peer, 1 - core, d).wait_recv()
+    advance(jnp.int32(0))
+    for d, peer in enumerate(peers):
+        q_copy(me_t, d, peer).start()
+    for d, peer in enumerate(peers):
+        h_copy(me_t, d, 1, peer).start()
+
+    @pl.loop(1, AHEAD)
+    def _(step):
+        advance(step)
+
+    own[2].wait()
+    own[3].wait()
+    for d, peer in enumerate(peers):
+        q_copy(peer, d, peer).wait_recv()
+    for part in range(2, CHUNKS):
         for d, peer in enumerate(peers):
-            h_copy(peer, d, part, peer).wait_recv()
-        vec = jnp.zeros((chunk_rows, feats), jnp.float32)
-        for t in range(tp):
-            vec = vec + jnp.dot(
-                hbuf[t, part].reshape(chunk_rows, hbuf.shape[-1]), wbuf[t],
-                preferred_element_type=jnp.float32,
-            )
-        table[me_c * CHUNKS + part] = vec.astype(jnp.bfloat16)
-        hand_on(at_a, at_b, part, lambda copy: copy.start())
-
-    own[1].wait()
-    for d, peer in enumerate(peers):
-        q_copy(peer, d, peer).wait_recv()
+            h_copy(me_t, d, part, peer).start()
     for t in range(tp):
         qfull[:, t * width:(t + 1) * width] = qbuf[t]
-    for row in range(stat_rows):
-        rows = slice(row * LANES, (row + 1) * LANES)
-        product = qbuf[me_t, rows, :].astype(jnp.float32) * pos_ref[rows, :].astype(jnp.float32)
-        stats[me_t, stat_rows + row:stat_rows + row + 1, :] = as_row(
-            jnp.sum(product, axis=1, keepdims=True)
-        )
-
-    def attend(slot):
-        items = table[slot]
-        for g in range(groups):
+
+    def attend(pair, wanted):
+        items = table[pair].reshape(2 * chunk_rows, feats)
+        for g in wanted:
             rows = slice(g * BLK, (g + 1) * BLK)
             raw = lax.dot_general(
                 qfull[rows, :], items, (((1,), (1,)), ((), ())), preferred_element_type=jnp.float32
             )
             tiles = [
-                raw[:, i * LANES:(i + 1) * LANES] * (scale * LOG2E) + bias_ref[g, slot, i:i + 1, :]
-                for i in range(chunk_rows // LANES)
+                raw[:, i * LANES:(i + 1) * LANES] * (scale * LOG2E) + bias_ref[g, pair, i:i + 1, :]
+                for i in range(2 * chunk_rows // LANES)
             ]
             top = functools.reduce(jnp.maximum, tiles)
             old_max = run_max[rows, :]
@@ -198,37 +255,23 @@
                 cols = slice(i * LANES, (i + 1) * LANES)
                 acc[rows, cols] = acc[rows, cols] * fade + part[:, cols]
 
-    ranks = sorted(
-        [(i, j) for i in range(rows_a) for j in range(rows_b)], key=lambda r: (r[0] + r[1], r[1])
-    )
-    near_a, near_b = nearest(rows_a), nearest(rows_b)
-
-    def source(index):
-        rank_a = lookup(index, [r[0] for r in ranks])
-        rank_b = lookup(index, [r[1] for r in ranks])
-        a = lookup(rank_a * rows_a + at_a, [near_a[p][r] for r in range(rows_a) for p in range(rows_a)])
-        b = lookup(rank_b * rows_b + at_b, [near_b[p][r] for r in range(rows_b) for p in range(rows_b)])
-        return a, b
-
-    @pl.loop(0, len(ranks) * CHUNKS)
+    steps = len(order)
+
+    @pl.loop(0, steps - 1)
     def _(step):
-        index, part = step // CHUNKS, step % CHUNKS
-        a, b = source(index)
-
-        @pl.when(index > 0)
+        @pl.when(step + AHEAD < steps)
         def _():
-            table_copy(cat_of(a, b, core) * CHUNKS + part, 4).wait_recv()
-            hand_on(a, b, part, lambda copy: copy.start())
-
-        @pl.loop(0, 2)
-        def _(other):
-            slot = cat_of(a, b, (core + other) % 2) * CHUNKS + part
-
-            @pl.when(other > 0)
-            def _():
-                table_copy(slot, 4).wait_recv()
-
-            attend(slot)
+            advance(step + AHEAD)
+
+        attend(partner(step), range(groups))
+
+    for row in range(stat_rows):
+        rows = slice(row * LANES, (row + 1) * LANES)
+        product = qbuf[me_t, rows, :].astype(jnp.float32) * pos_ref[rows, :].astype(jnp.float32)
+        stats[me_t, stat_rows + row:stat_rows + row + 1, :] = as_row(
+            jnp.sum(product, axis=1, keepdims=True)
+        )
+    last = partner(jnp.int32(steps - 1))
 
     def o_copy(slot, d, g, peer):
         rows = pl.ds(g * BLK, BLK)
@@ -238,6 +281,7 @@
         return across(stats.at[slot], stats.at[slot], s_send.at[d], s_recv.at[slot], peer)
 
     for g in range(groups):
+        attend(last, [g])
         rows = slice(g * BLK, (g + 1) * BLK)
         norm = jnp.sum(run_sum[rows, :], axis=1, keepdims=True)
         lse = run_max[rows, 0:1] + jnp.log2(norm)
@@ -278,6 +322,7 @@
 
     for d, peer in enumerate(peers):
         w_copy(me_t, d, peer).wait_send()
+        w_hand(peer, core, d).wait_send()
         q_copy(me_t, d, peer).wait_send()
         for part in range(CHUNKS):
             h_copy(me_t, d, part, peer).wait_send()
@@ -285,11 +330,9 @@
             o_copy(me_t, d, g, peer).wait_send()
         s_copy(me_t, d, peer).wait_send()
 
-    @pl.loop(0, len(ranks) * CHUNKS)
+    @pl.loop(0, steps)
     def _(step):
-        index, part = step // CHUNKS, step % CHUNKS
-        a, b = source(index)
-        hand_on(a, b, part, lambda copy: copy.wait_send())
+        hand_on(*source(step), lambda copy: copy.wait_send())
 
 
 def local(query_emb, positive_emb, item_hidden, item_weight, neg_blocks, block_home, sample_counts):
@@ -305,7 +348,7 @@
     total_blocks = block_home.shape[0]
     groups = neg_blocks.shape[0]
     chunk_rows = own_blocks * sub_rows // CHUNKS
-    slots = cats * CHUNKS
+    pairs = cats // 2 * CHUNKS
     scale = 2.0 / math.sqrt(feats)
 
     ids = jnp.arange(total_blocks, dtype=jnp.int32)
@@ -313,27 +356,31 @@
     stored = jnp.any(chosen[:, :, None] & (block_home[:, None] == ids), axis=1)
     log_q = jnp.log(sample_counts.astype(jnp.float32)).reshape(total_blocks, tp, sub_rows)
     log_q = lax.dynamic_index_in_dim(log_q, me_t, 1, keepdims=False)
-    bias = jnp.where(stored[:, :, None], log_q * -LOG2E, NEG).reshape(
-        groups, slots, chunk_rows // LANES, LANES
+    bias = jnp.where(stored[:, :, None], log_q * -LOG2E, NEG)
+    bias = (
+        bias.reshape(groups, cats // 2, 2, CHUNKS, chunk_rows)
+        .transpose(0, 1, 3, 2, 4)
+        .reshape(groups, pairs, 2 * chunk_rows // LANES, LANES)
     )
     vmem = pl.BlockSpec(memory_space=pltpu.VMEM)
     hbm = pl.BlockSpec(memory_space=pl.ANY)
     dma = pltpu.SemaphoreType.DMA
     others = max(tp - 1, 1)
-    flops = 4 * queries * slots * chunk_rows * feats
+    pairwise = queries * pairs * 2 * chunk_rows
     loss, grad = pl.pallas_call(
         functools.partial(kernel, (tp, rows_a, rows_b), scale),
         out_shape=(
             jax.ShapeDtypeStruct((queries // LANES, LANES), jnp.float32),
             jax.ShapeDtypeStruct((queries, width), jnp.bfloat16),
         ),
-        in_specs=[hbm, vmem, hbm, hbm, vmem],
+        in_specs=[hbm, hbm, hbm, hbm, vmem],
         out_specs=(vmem, vmem),
         scratch_shapes=[
-            pltpu.VMEM((slots, chunk_rows, feats), jnp.bfloat16),
+            pltpu.VMEM((pairs, 2, chunk_rows, feats), jnp.bfloat16),
             pltpu.VMEM((tp, CHUNKS, own_blocks // CHUNKS, sub_rows, hid), jnp.bfloat16),
-            pltpu.VMEM((tp, hid, feats), jnp.bfloat16),
+            pltpu.VMEM((tp, 2, hid // 2, feats), jnp.bfloat16),
             pltpu.VMEM((tp, queries, width), jnp.bfloat16),
+            pltpu.VMEM((queries, width), jnp.bfloat16),
             pltpu.VMEM((queries, feats), jnp.bfloat16),
             pltpu.VMEM((queries, LANES), jnp.float32),
             pltpu.VMEM((queries, LANES), jnp.float32),
@@ -341,19 +388,19 @@
             pltpu.VMEM((others, queries, width), jnp.bfloat16),
             pltpu.VMEM((tp, queries, width), jnp.bfloat16),
             pltpu.VMEM((tp, 2 * queries // LANES, LANES), jnp.float32),
-            dma((2 + CHUNKS,)),
-            dma((others,)), dma((tp,)),
+            dma((4 + CHUNKS,)),
+            dma((others,)), dma((tp, 2)), dma((others,)),
             dma((others,)), dma((tp,)),
             dma((others, CHUNKS)), dma((tp, CHUNKS)),
-            dma((slots, 5)), dma((slots,)),
+            dma((pairs, 5)), dma((pairs, 2)),
             dma((others, groups)), dma((tp, groups)),
             dma((others,)), dma((tp,)),
         ],
         compiler_params=pltpu.CompilerParams(
-            collective_id=0, has_side_effects=True, vmem_limit_bytes=48 * 1024 * 1024
+            collective_id=0, has_side_effects=True, vmem_limit_bytes=60 * 1024 * 1024
         ),
         cost_estimate=pl.CostEstimate(
-            flops=flops, bytes_accessed=8 * 1024 * 1024, transcendentals=queries * slots * chunk_rows
+            flops=4 * pairwise * feats, bytes_accessed=8 * 1024 * 1024, transcendentals=pairwise
         ),
     )(
         query_emb, positive_emb, item_hidden.reshape(own_blocks, BLK, hid), item_weight, bias,

time: 169 us -> 168 us (level)
  Pallas kernels: 158 us -> 160 us
  local copies, waits for them, and re-layouts: 6.23 us -> 4.5 us
    unnamed x10 -> x2, local copies, waits for them, and re-layouts: 6.1 us -> 3.14 us
where the time goes in v2:
time: 168 us
  Pallas kernels  160 us (95%)
  local copies, waits for them, and re-layouts  4.5 us (3%)
  other arithmetic  2.93 us (2%)
    pallas_call x1, Pallas kernels, local(): pl.pallas_call(functools.partial(kernel, (tp, rows_a, rows_b), scale), ou...  160 us

profile of v2, /device:TPU:0, one launch (start us, length us, event | category | flops | bytes accessed | tf_op | source)
XLA Modules:
  0.0 167.8 jit_solution(11956380911751122997)
XLA Ops:
  0.6 0.8 fusion
  1.4 0.7 iota_compare_fusion.1
  2.2 0.1 and_reduce_fusion
  2.3 0.1 broadcast_in_dim.25
  2.5 0.1 broadcast_in_dim.26
  2.6 0.9 convert_log_fusion
  3.5 0.2 multiply_reduce_fusion
  3.8 0.1 select_bitcast_fusion
  3.9 0.1 copy.11
  4.0 1.0 reshape.45.bias_ref
  5.0 159.6 %shard_map.86 = (f32[8,128]{1,0:T(8,128)}, bf16[1024,256]{1,0:T(8,128)(2,1)}) custom-call(bf16[1024,256]{1,0:T(8,128)(2,1)} %q_ref.1, bf16[1024,256]{1,0:T(8,128)(2,1)} %pos_in.1, bf16[8,256,512]{2,1,0:T(8,128)(2,1)} %bitcast.7, bf16[512,512]{1,0:T(8,128)(2,1)} %w_ref.1, f32[4,32,4,128]{3,2,1,0:T(4,128)} %reshape.45.bias_ref), custom_call_target="tpu_custom_call" | custom-call | flops 34359738368 | bytes 8388608 | tf_op jit(solution)/shard_map/pallas_call | solution.py:370
  164.6 1.3 copy.14
  165.9 1.9 %copy.15 = bf16[1024,256]{1,0:T(8,128)(2,1)} copy(bf16[1024,256]{1,0:T(8,128)(2,1)} %get-tuple-element.9) | data formatting | bytes 1048576
  (1 shorter events, 0.0 us)

commit v3 on v2

--- a/solution.py
+++ b/solution.py
@@ -31,7 +31,7 @@
 def kernel(
     sizes, scale,
     q_ref, pos_in, h_ref, w_ref, bias_ref, loss_ref, grad_ref,
-    table, hbuf, wbuf, qbuf, pos_ref, qfull, run_max, run_sum, acc, osend, orecv, stats,
+    table, hbuf, wbuf, qbuf, pos_ref, qfull, raw_even, raw_odd, weights, run_max, run_sum, acc, osend, orecv, stats,
     local_sem, w_send, w_recv, w_pass, q_send, q_recv, h_send, h_recv,
     t_send, t_recv, o_send, o_recv, s_send, s_recv,
 ):
@@ -231,15 +231,18 @@
     for t in range(tp):
         qfull[:, t * width:(t + 1) * width] = qbuf[t]
 
-    def attend(pair, wanted):
+    def score(pair, raw):
         items = table[pair].reshape(2 * chunk_rows, feats)
-        for g in wanted:
+        raw[...] = lax.dot_general(
+            qfull[...], items, (((1,), (1,)), ((), ())), preferred_element_type=jnp.float32
+        )
+
+    def absorb(pair, raw):
+        fades = []
+        for g in range(groups):
             rows = slice(g * BLK, (g + 1) * BLK)
-            raw = lax.dot_general(
-                qfull[rows, :], items, (((1,), (1,)), ((), ())), preferred_element_type=jnp.float32
-            )
             tiles = [
-                raw[:, i * LANES:(i + 1) * LANES] * (scale * LOG2E) + bias_ref[g, pair, i:i + 1, :]
+                raw[rows, i * LANES:(i + 1) * LANES] * (scale * LOG2E) + bias_ref[g, pair, i:i + 1, :]
                 for i in range(2 * chunk_rows // LANES)
             ]
             top = functools.reduce(jnp.maximum, tiles)
@@ -249,29 +252,44 @@
             tiles = [jnp.exp2(tile - new_max) for tile in tiles]
             run_max[rows, :] = new_max
             run_sum[rows, :] = run_sum[rows, :] * fade + functools.reduce(jnp.add, tiles)
-            weights = jnp.concatenate([tile.astype(jnp.bfloat16) for tile in tiles], axis=1)
-            part = jnp.dot(weights, items, preferred_element_type=jnp.float32)
+            for i, tile in enumerate(tiles):
+                weights[rows, i * LANES:(i + 1) * LANES] = tile.astype(jnp.bfloat16)
+            fades.append(fade)
+        items = table[pair].reshape(2 * chunk_rows, feats)
+        part = jnp.dot(weights[...], items, preferred_element_type=jnp.float32)
+        for g in range(groups):
+            rows = slice(g * BLK, (g + 1) * BLK)
             for i in range(feats // LANES):
                 cols = slice(i * LANES, (i + 1) * LANES)
-                acc[rows, cols] = acc[rows, cols] * fade + part[:, cols]
+                acc[rows, cols] = acc[rows, cols] * fades[g] + part[rows, cols]
 
     steps = len(order)
 
-    @pl.loop(0, steps - 1)
-    def _(step):
-        @pl.when(step + AHEAD < steps)
-        def _():
-            advance(step + AHEAD)
-
-        attend(partner(step), range(groups))
-
+    first = partner(jnp.int32(0))
+    score(first, raw_even)
+
+    @pl.loop(0, steps // 2 - 1)
+    def _(twice):
+        step = twice * 2
+        for later, raw, raw_next in ((0, raw_even, raw_odd), (1, raw_odd, raw_even)):
+            @pl.when(step + later + AHEAD < steps)
+            def _():
+                advance(step + later + AHEAD)
+
+            coming = partner(step + later + 1)
+            score(coming, raw_next)
+            absorb(pair_of(*source(step + later)), raw)
+
+    last = partner(jnp.int32(steps - 1))
+    score(last, raw_odd)
+    absorb(pair_of(*source(jnp.int32(steps - 2))), raw_even)
     for row in range(stat_rows):
         rows = slice(row * LANES, (row + 1) * LANES)
         product = qbuf[me_t, rows, :].astype(jnp.float32) * pos_ref[rows, :].astype(jnp.float32)
         stats[me_t, stat_rows + row:stat_rows + row + 1, :] = as_row(
             jnp.sum(product, axis=1, keepdims=True)
         )
-    last = partner(jnp.int32(steps - 1))
+    absorb(last, raw_odd)
 
     def o_copy(slot, d, g, peer):
         rows = pl.ds(g * BLK, BLK)
@@ -281,7 +299,6 @@
         return across(stats.at[slot], stats.at[slot], s_send.at[d], s_recv.at[slot], peer)
 
     for g in range(groups):
-        attend(last, [g])
         rows = slice(g * BLK, (g + 1) * BLK)
         norm = jnp.sum(run_sum[rows, :], axis=1, keepdims=True)
         lse = run_max[rows, 0:1] + jnp.log2(norm)
@@ -382,6 +399,9 @@
             pltpu.VMEM((tp, queries, width), jnp.bfloat16),
             pltpu.VMEM((queries, width), jnp.bfloat16),
             pltpu.VMEM((queries, feats), jnp.bfloat16),
+            pltpu.VMEM((queries, 2 * chunk_rows), jnp.float32),
+            pltpu.VMEM((queries, 2 * chunk_rows), jnp.float32),
+            pltpu.VMEM((queries, 2 * chunk_rows), jnp.bfloat16),
             pltpu.VMEM((queries, LANES), jnp.float32),
             pltpu.VMEM((queries, LANES), jnp.float32),
             pltpu.VMEM((queries, feats), jnp.float32),

time: 168 us -> 164 us (0.976)
  Pallas kernels: 160 us -> 156 us
    pallas_call x1, Pallas kernels: 160 us -> 156 us  [local(): pl.pallas_call(functools.partial(kernel, (tp, rows_a, rows_b), scale), ou...]
where the time goes in v3:
time: 164 us
  Pallas kernels  156 us (95%)
  local copies, waits for them, and re-layouts  4.5 us (3%)
  other arithmetic  2.93 us (2%)
    pallas_call x1, Pallas kernels, local(): pl.pallas_call(functools.partial(kernel, (tp, rows_a, rows_b), scale), ou...  156 us

profile of v3, /device:TPU:0, one launch (start us, length us, event | category | flops | bytes accessed | tf_op | source)
XLA Modules:
  0.0 163.8 jit_solution(16283832602464532425)
XLA Ops:
  0.6 0.8 fusion
  1.4 0.7 iota_compare_fusion.1
  2.2 0.1 and_reduce_fusion
  2.3 0.1 broadcast_in_dim.25
  2.5 0.1 broadcast_in_dim.26
  2.6 0.9 convert_log_fusion
  3.5 0.2 multiply_reduce_fusion
  3.8 0.1 select_bitcast_fusion
  3.9 0.1 copy.11
  4.0 1.0 reshape.45.bias_ref
  5.0 155.7 %shard_map.86 = (f32[8,128]{1,0:T(8,128)}, bf16[1024,256]{1,0:T(8,128)(2,1)}) custom-call(bf16[1024,256]{1,0:T(8,128)(2,1)} %q_ref.1, bf16[1024,256]{1,0:T(8,128)(2,1)} %pos_in.1, bf16[8,256,512]{2,1,0:T(8,128)(2,1)} %bitcast.7, bf16[512,512]{1,0:T(8,128)(2,1)} %w_ref.1, f32[4,32,4,128]{3,2,1,0:T(4,128)} %reshape.45.bias_ref), custom_call_target="tpu_custom_call" | custom-call | flops 34359738368 | bytes 8388608 | tf_op jit(solution)/shard_map/pallas_call | solution.py:387
  160.7 1.3 copy.14
  162.0 1.9 %copy.15 = bf16[1024,256]{1,0:T(8,128)(2,1)} copy(bf16[1024,256]{1,0:T(8,128)(2,1)} %get-tuple-element.9) | data formatting | bytes 1048576
  (1 shorter events, 0.0 us)

commit v4 on v3

--- a/solution.py
+++ b/solution.py
@@ -144,21 +144,19 @@
             device_id={"cat": ways[way][1]}, device_id_type=pl.DeviceIdType.MESH,
         )
 
-    def sends(a, b, part):
-        b_first = (part == 2) & (a != rows_a // 2)
-        along_a = b_first | (b == at_b)
-        along_b = jnp.logical_not(b_first) | (a == at_a)
+    def sends(a, b):
+        along_a = b == at_b
         return [
             ways[0][0] & along_a & (a >= at_a),
             ways[1][0] & along_a & (a <= at_a),
-            ways[2][0] & along_b & (b >= at_b),
-            ways[3][0] & along_b & (b <= at_b),
+            ways[2][0] & (b >= at_b),
+            ways[3][0] & (b <= at_b),
             ways[4][0],
         ]
 
     def hand_on(a, b, part, act):
         pair = pair_of(a, b, part)
-        for way, wanted in enumerate(sends(a, b, part)):
+        for way, wanted in enumerate(sends(a, b)):
             @pl.when(wanted)
             def _():
                 act(table_copy(pair, core, way))

time: 164 us -> 162 us (0.988)
  Pallas kernels: 156 us -> 153 us
    pallas_call x1, Pallas kernels: 156 us -> 153 us  [local(): pl.pallas_call(functools.partial(kernel, (tp, rows_a, rows_b), scale), ou...]
where the time goes in v4:
time: 162 us
  Pallas kernels  153 us (94%)
  local copies, waits for them, and re-layouts  4.5 us (3%)
  other arithmetic  2.93 us (2%)
    pallas_call x1, Pallas kernels, local(): pl.pallas_call(functools.partial(kernel, (tp, rows_a, rows_b), scale), ou...  153 us

profile of v4, /device:TPU:0, one launch (start us, length us, event | category | flops | bytes accessed | tf_op | source)
XLA Modules:
  0.0 161.6 jit_solution(13232211877931488239)
XLA Ops:
  0.6 0.8 fusion
  1.4 0.7 iota_compare_fusion.1
  2.2 0.1 and_reduce_fusion
  2.3 0.1 broadcast_in_dim.25
  2.5 0.1 broadcast_in_dim.26
  2.6 0.9 convert_log_fusion
  3.5 0.2 multiply_reduce_fusion
  3.8 0.1 select_bitcast_fusion
  3.9 0.1 copy.11
  4.0 1.0 reshape.45.bias_ref
  5.0 153.5 %shard_map.86 = (f32[8,128]{1,0:T(8,128)}, bf16[1024,256]{1,0:T(8,128)(2,1)}) custom-call(bf16[1024,256]{1,0:T(8,128)(2,1)} %q_ref.1, bf16[1024,256]{1,0:T(8,128)(2,1)} %pos_in.1, bf16[8,256,512]{2,1,0:T(8,128)(2,1)} %bitcast.7, bf16[512,512]{1,0:T(8,128)(2,1)} %w_ref.1, f32[4,32,4,128]{3,2,1,0:T(4,128)} %reshape.45.bias_ref), custom_call_target="tpu_custom_call" | custom-call | flops 34359738368 | bytes 8388608 | tf_op jit(solution)/shard_map/pallas_call | solution.py:385
  158.5 1.3 copy.14
  159.7 1.9 %copy.15 = bf16[1024,256]{1,0:T(8,128)(2,1)} copy(bf16[1024,256]{1,0:T(8,128)(2,1)} %get-tuple-element.9) | data formatting | bytes 1048576
  (1 shorter events, 0.0 us)
